TPU v7x, 32 devices: a whole 2x2x4 slice. The times are simulated.
32 devices in a mesh: fsdp: 16 (over z, x, core), tensor: 2 (over y).
Axes of the slice: x: 2, y: 2, z: 4, core: 2. Of those that a mesh axis runs over, the one named last changes fastest.
Arguments:
- grad: bfloat16 [16384, 8192], P('tensor', 'fsdp'), may hold values from -0.26953125 to 0.26953125
- owner: int32 [4, 8], replicated, may hold values from 0 to 7, each once within a row
- codes: int32 [2, 16384, 8192], P(None, 'tensor', 'fsdp'), may hold values from 0 to 15
- scale_ids: int32 [2, 128, 8192], P(None, 'tensor', 'fsdp'), may hold values from 0 to 15
- scale_table: float32 [16], replicated, may hold values from 0.1 to 1
Outputs:
- statistics: float32 [2, 16384, 8192], P(None, 'tensor', 'fsdp')
Inputs may be any that keep to these rules, and one draw needn't show every extreme that they name: Each row owner[c] holds every slot 0 to 7 once: block row r of block column c keeps its statistics at slot owner[c, r].
All inputs are finite; a program needn't handle non-finite values.
Results may differ from a plain program's by a relative error of at most 0.0003.
Values may be sent and summed in bfloat16 or wider, within the bound.
A program may use at most 192 MiB of HBM per device.

v0:
```python
import jax
import jax.numpy as jnp
from jax import lax
from jax.sharding import PartitionSpec as P

B = 2048


def partner_2(value, axis, bit):
    mask = 2**bit
    pairs = [(source, source ^ mask) for source in range(lax.axis_size(axis))]
    return lax.ppermute(value, axis, pairs)


def left_part(slab_piece, member, piece_width):
    own_rows = lax.dynamic_slice_in_dim(slab_piece, member * piece_width, piece_width, 1)
    return jnp.einsum("sbj,scj->sbc", slab_piece, own_rows, preferred_element_type=jnp.float32)


def right_part(slab_piece, own_piece):
    return jnp.einsum("sbj,sbc->sjc", slab_piece, own_piece, preferred_element_type=jnp.float32)


def shards(grad, owner, codes, scale_ids, scale_table):
    rows_here = grad.shape[0]
    width_here = grad.shape[1]
    slot_count = rows_here // B
    tensor_count = lax.axis_size("tensor")
    group_size = B // width_here
    tensor_pos = lax.axis_index("tensor")
    fsdp_pos = lax.axis_index("fsdp")
    column_block = fsdp_pos // group_size
    member = fsdp_pos % group_size
    owner_row = lax.dynamic_index_in_dim(owner, column_block, 0, keepdims=False)
    pieces = grad.reshape(slot_count, B, width_here)
    local_slots = lax.dynamic_slice_in_dim(owner_row, tensor_pos * slot_count, slot_count)
    targets = jnp.arange(tensor_count * slot_count, dtype=jnp.int32).reshape(
        tensor_count, slot_count
    )
    select = (targets[:, :, None] == local_slots[None, None, :]).astype(jnp.bfloat16)
    outgoing = jnp.einsum(
        "dsr,rbc->dsbc", select, pieces, preferred_element_type=jnp.float32
    ).astype(jnp.bfloat16)
    incoming = lax.all_to_all(outgoing, "tensor", split_axis=0, concat_axis=0, tiled=True)
    owned_block = jnp.sum(incoming, axis=0, dtype=jnp.float32).astype(jnp.bfloat16)
    depth_count = group_size.bit_length() - 1
    collected = owned_block
    for step_bit in range(depth_count):
        partner = partner_2(collected, "fsdp", step_bit)
        upper_half = fsdp_pos // (1 << step_bit) % 2 == 1
        collected = jnp.where(
            upper_half,
            jnp.concatenate([partner, collected], 2),
            jnp.concatenate([collected, partner], 2),
        )
    left_gram = left_part(collected, member, width_here)
    right_gram = right_part(collected, owned_block)
    stacked = jnp.stack(
        [left_gram.reshape(rows_here, width_here), right_gram.reshape(rows_here, width_here)]
    )
    group_rows = rows_here // scale_ids.shape[1]
    level_index = jnp.arange(scale_table.shape[0], dtype=jnp.int32)
    scale_grid = jnp.sum(jnp.where(scale_ids[..., None] == level_index, scale_table, 0.0), axis=-1)
    previous = scale_grid[:, :, None, :] * (
        (codes.reshape(2, -1, group_rows, width_here).astype(jnp.float32) - 7.5) / 7.5
    )
    previous = previous.reshape(2, rows_here, width_here)
    return 0.9 * previous + 0.1 * stacked


def solution(mesh):
    in_specs = (P("tensor", "fsdp"), P(), P(None, "tensor", "fsdp"), P(None, "tensor", "fsdp"), P())
    out_specs = P(None, "tensor", "fsdp")
    return jax.shard_map(shards, mesh=mesh, in_specs=in_specs, out_specs=out_specs, check_vma=False)
```

profile of v0, /device:TPU:0, one launch (start us, length us, event | category | flops | bytes accessed | tf_op | source)
XLA Modules:
  0.0 750.2 jit_solution(8630264579725261185)
XLA Ops:
  0.0 0.0 copy-start
  0.0 0.7 copy-done
  0.7 0.1 dynamic-slice_bitcast_fusion
  0.8 12.6 %convolution_convert_fusion = bf16[2,4,2048,512]{3,1,2,0:T(4,128)(2,1)S(1)} fusion(bf16[4,2048,512]{2,1,0:T(8,128)(2,1)} %bitcast.23, s32[4]{0:T(128)S(1)} %dynamic-slice_bitcast_fusion, s32[2,4]{1,0:T(2,128)S(1)} %multiply_add_fusion), kind=kOutput, calls=%fused_computation.6 | convolution fusion | flops 75497504 | bytes 25165872 | tf_op jit(solution)/shard_map/dsr,rbc->dsbc/dot_general | solution.py:41
  13.4 189.4 %all_to_all.5 = bf16[2,4,2048,512]{3,1,2,0:T(4,128)(2,1)} all-to-all(bf16[2,4,2048,512]{3,1,2,0:T(4,128)(2,1)S(1)} %convolution_convert_fusion), channel_id=1, replica_groups=mesh['fsdp'=16,'tensor'=2] {'tensor'}, dimensions={0} | all-to-all | bytes 33554432 | tf_op jit(solution)/shard_map/all_to_all | solution.py:44
  202.8 0.0 copy-start.2
  202.8 0.0 copy-start.3
  202.8 19.2 %reduce_sum.22 = bf16[4,2048,512]{2,0,1:T(4,128)(2,1)} reduce(bf16[2,4,2048,512]{3,1,2,0:T(4,128)(2,1)} %all_to_all.5, bf16[]{:T(256)} %constant.95.clone.1), dimensions={0}, to_apply=%region_1.2 | reduce | flops 4194304 | bytes 25165826 | tf_op jit(solution)/shard_map/reduce_sum | solution.py:45
  222.1 8.5 %copy.15 = bf16[4,2048,512]{2,1,0:T(8,128)(2,1)} copy(bf16[4,2048,512]{2,0,1:T(4,128)(2,1)} %reduce_sum.22) | data formatting | bytes 16777216 | tf_op jit(solution)/shard_map/reduce_sum | solution.py:45
  230.5 0.0 collective-permute-start
  230.5 13.5 %collective-permute-done = bf16[4,2048,512]{2,1,0:T(8,128)(2,1)} collective-permute-done((bf16[4,2048,512]{2,1,0:T(8,128)(2,1)}, bf16[4,2048,512]{2,1,0:T(8,128)(2,1)}, u32[]{:S(2)}, u32[]{:S(2)}) %collective-permute-start) | collective-permute-done | bytes 8388640 | tf_op jit(solution)/shard_map/ppermute | solution.py:12
  244.0 20.6 %maximum_select_fusion.1 = bf16[4,2048,1024]{2,1,0:T(8,128)(2,1)} fusion(bf16[4,2048,512]{2,1,0:T(8,128)(2,1)} %copy.15, bf16[4,2048,512]{2,1,0:T(8,128)(2,1)} %collective-permute-done, pred[]{:T(512)S(6)} %eq.42), kind=kLoop, calls=%fused_computation.5 | loop fusion | flops 75497472 | bytes 33554432 | tf_op jit(solution)/shard_map/jit(_where)/select_n | solution.py:51
  264.7 1.5 collective-permute-start.1
  266.2 0.0 copy-done.2
  266.2 0.0 copy-done.3
  266.2 1.3 select_reduce_fusion
  267.6 359.7 %collective-permute-done.1 = bf16[4,2048,1024]{2,1,0:T(8,128)(2,1)} collective-permute-done((bf16[4,2048,1024]{2,1,0:T(8,128)(2,1)}, bf16[4,2048,1024]{2,1,0:T(8,128)(2,1)}, u32[]{:S(2)}, u32[]{:S(2)}) %collective-permute-start.1) | collective-permute-done | bytes 16777248 | tf_op jit(solution)/shard_map/ppermute | solution.py:12
  627.3 34.3 %maximum_select_fusion = bf16[4,2048,2048]{2,1,0:T(8,128)(2,1)} fusion(bf16[4,2048,1024]{2,1,0:T(8,128)(2,1)} %maximum_select_fusion.1, bf16[4,2048,1024]{2,1,0:T(8,128)(2,1)} %collective-permute-done.1, pred[]{:T(512)S(6)} %eq.41), kind=kLoop, calls=%fused_computation | loop fusion | flops 150994944 | bytes 67108864 | tf_op jit(solution)/shard_map/jit(_where)/select_n | solution.py:51
  661.6 27.3 %fusion.11 = f32[4,2048,512]{2,1,0:T(8,128)} fusion(bf16[4,2048,2048]{2,1,0:T(8,128)(2,1)} %maximum_select_fusion, bf16[4,2048,512]{2,0,1:T(4,128)(2,1)} %reduce_sum.22), kind=kOutput, calls=%fused_computation.21 | convolution fusion | flops 17179869184 | bytes 58720256 | tf_op jit(solution)/shard_map/sbj,sbc->sjc/dot_general | solution.py:21
  688.9 27.5 %fusion.4 = f32[4,2048,512]{2,1,0:T(8,128)} fusion(bf16[4,2048,2048]{2,1,0:T(8,128)(2,1)} %maximum_select_fusion, s32[]{:T(128)S(6)} %select_n.71), kind=kOutput, calls=%fused_computation.9 | convolution fusion | flops 17179869184 | bytes 58720260 | tf_op jit(solution)/shard_map/sbj,scj->sbc/dot_general | solution.py:17
  716.4 0.0 copy-start.1
  716.4 33.7 %fusion = f32[2,8192,512]{2,1,0:T(8,128)} fusion(f32[1,8192,512]{2,1,0:T(8,128)} %bitcast.21, f32[1,8192,512]{2,1,0:T(8,128)} %bitcast.22, s32[2,8192,512]{2,1,0:T(8,128)} %param.7, f32[2,64,512]{2,1,0:T(8,128)S(1)} %broadcast_multiply_fusion), kind=kLoop, calls=%fused_computation.2 | loop fusion | flops 58720256 | bytes 100925440 | tf_op jit(solution)/shard_map/add | solution.py:68
  750.2 0.0 copy-done.1
  (2 shorter events, 0.0 us)
Async XLA Ops:
  0.0 0.7 copy-start
  202.8 63.4 %copy-start.2 = (s32[2,64,512]{2,1,0:T(8,128)S(1)}, s32[2,64,512]{2,1,0:T(8,128)}, u32[]{:S(2)}) copy-start(s32[2,64,512]{2,1,0:T(8,128)} %param.8) | copy-start | bytes 786436
  202.8 63.4 %copy-start.3 = (f32[16]{0:T(128)S(1)}, f32[16]{0:T(128)}, u32[]{:S(2)}) copy-start(f32[16]{0:T(128)} %param.9) | copy-start | bytes 196
  230.5 13.5 %collective-permute-start = (bf16[4,2048,512]{2,1,0:T(8,128)(2,1)}, bf16[4,2048,512]{2,1,0:T(8,128)(2,1)}, u32[]{:S(2)}, u32[]{:S(2)}) collective-permute-start(bf16[4,2048,512]{2,1,0:T(8,128)(2,1)} %copy.15), channel_id=1, source_target_pairs={{0,2},{2,0},{4,6},{6,4},{8,10},{10,8},{12,14},{14,12},{16,18},{18,... | collective-permute-start | bytes 25165832 | tf_op jit(solution)/shard_map/ppermute | solution.py:12
  264.7 362.6 %collective-permute-start.1 = (bf16[4,2048,1024]{2,1,0:T(8,128)(2,1)}, bf16[4,2048,1024]{2,1,0:T(8,128)(2,1)}, u32[]{:S(2)}, u32[]{:S(2)}) collective-permute-start(bf16[4,2048,1024]{2,1,0:T(8,128)(2,1)} %maximum_select_fusion.1), channel_id=1, source_target_pairs={{0,4},{2,6},{4,0},{6,2},{8,12},{10,14},{12,8},{14,10},{16,20},{18,... | collective-permute-start | bytes 50331656 | tf_op jit(solution)/shard_map/ppermute | solution.py:12
  716.4 33.8 %copy-start.1 = (s32[4,8]{1,0:T(4,128)S(1)}, s32[4,8]{1,0:T(4,128)}, u32[]{:S(2)}) copy-start(s32[4,8]{1,0:T(4,128)} %param.6) | copy-start | bytes 388
where the time goes:
time: 751 us; the launch traced here: 750 us
  waiting for transfers between devices  373 us (50%)
  blocking collectives  189 us (25%)
  other arithmetic  109 us (15%)
  matrix products  67.4 us (9%)
  local copies, waits for them, and re-layouts  9.23 us (1%)
    ppermute x2, waiting for transfers between devices, partner_2(): return lax.ppermute(value, axis, pairs)  373 us
    all_to_all x1, blocking collectives, shards(): lax.all_to_all(outgoing, 'tensor', split_axis=0, concat_axis=0, tiled=True)  189 us
    select_n x2, other arithmetic, shards(): jnp.where(upper_half, jnp.concatenate([partner, collected], 2), jnp.conca...  55 us
    add x1, other arithmetic, shards(): return 0.9 * previous + 0.1 * stacked  33.7 us
    dot_general x1, matrix products, left_part(): jnp.einsum('sbj,scj->sbc', slab_piece, own_rows, preferred_element_type=j...  27.5 us
    dot_general x1, matrix products, right_part(): jnp.einsum('sbj,sbc->sjc', slab_piece, own_piece, preferred_element_type=...  27.3 us
    reduce_sum x1, other arithmetic, shards(): jnp.sum(incoming, axis=0, dtype=jnp.float32).astype(jnp.bfloat16)  19.2 us
  transfers between devices with their start and end apart: 2, of which 2 were waited for; matrix products, arithmetic and copies ran while one was open for 0% of the time, Pallas kernels for 0%

commit v1 on v0

--- a/solution.py
+++ b/solution.py
@@ -1,6 +1,10 @@
+import functools
+
 import jax
 import jax.numpy as jnp
 from jax import lax
+from jax.experimental import pallas as pl
+from jax.experimental.pallas import tpu as pltpu
 from jax.sharding import PartitionSpec as P
 
 B = 2048
@@ -21,7 +25,7 @@
     return jnp.einsum("sbj,sbc->sjc", slab_piece, own_piece, preferred_element_type=jnp.float32)
 
 
-def shards(grad, owner, codes, scale_ids, scale_table):
+def general_shards(grad, owner, codes, scale_ids, scale_table):
     rows_here = grad.shape[0]
     width_here = grad.shape[1]
     slot_count = rows_here // B
@@ -68,7 +72,163 @@
     return 0.9 * previous + 0.1 * stacked
 
 
+def fold_kernel(levels, group_rows, aliased, place, table, *refs):
+    piece_refs = refs[:4]
+    codes, ids = refs[4:6]
+    out, scales = refs[-2:]
+    width = codes.shape[2]
+    half, tile = pl.program_id(0), pl.program_id(1)
+    member = place[1]
+
+    @pl.when(tile == 0)
+    def _():
+        wanted = ids[0]
+        found = jnp.zeros(wanted.shape, jnp.float32)
+        for level in range(levels):
+            found = jnp.where(wanted == level, table[level], found)
+        scales[...] = found * (0.9 / 7.5)
+
+    def blend(gram, out_tile):
+        for group in range(width // group_rows):
+            rows = pl.ds(group * group_rows, group_rows)
+            scale = scales[pl.ds(out_tile * (width // group_rows) + group, 1), :]
+            stored = scale * (codes[0, rows, :].astype(jnp.float32) - 7.5)
+            out[0, rows, :] = stored + 0.1 * gram[group * group_rows : (group + 1) * group_rows]
+
+    @pl.when(half == 0)
+    def _():
+        here = pl.ds(pl.multiple_of(tile * width, width), width)
+        own = pl.ds(pl.multiple_of(member * width, width), width)
+        gram = None
+        for piece in piece_refs:
+            term = lax.dot_general(
+                piece[here, :],
+                piece[own, :],
+                (((1,), (1,)), ((), ())),
+                preferred_element_type=jnp.float32,
+            )
+            gram = term if gram is None else gram + term
+        blend(gram, tile)
+
+    for position, piece in enumerate(piece_refs):
+
+        @pl.when((half == 1) & (tile == position))
+        def _():
+            gram = lax.dot_general(
+                piece[...],
+                piece_refs[0][...],
+                (((0,), (0,)), ((), ())),
+                preferred_element_type=jnp.float32,
+            )
+            blend(gram, lax.bitwise_xor(member, position))
+
+
+def fold(place, scale_table, pieces, codes, scale_ids, filled):
+    width = codes.shape[2]
+    tiles = B // width
+    id_rows = scale_ids.shape[1] // (codes.shape[1] // B)
+    group_rows = B // id_rows
+
+    def tile_of(half, tile, place, table):
+        placed = jnp.where(half == 0, tile, lax.bitwise_xor(place[1], tile))
+        return half, place[0] * tiles + placed, 0
+
+    def whole(half, tile, place, table):
+        return 0, 0
+
+    in_specs = [pl.BlockSpec((B, width), whole, pipeline_mode=pl.Buffered(1))] * len(pieces)
+    in_specs.append(pl.BlockSpec((1, width, width), tile_of))
+    in_specs.append(
+        pl.BlockSpec((1, id_rows, width), lambda half, tile, place, table: (half, place[0], 0))
+    )
+    operands = [place, scale_table, *pieces, codes, scale_ids]
+    aliases = {}
+    if filled is not None:
+        in_specs.append(pl.BlockSpec(memory_space=pl.ANY))
+        aliases = {len(operands): 0}
+        operands.append(filled)
+    return pl.pallas_call(
+        functools.partial(
+            fold_kernel, scale_table.shape[0], group_rows, filled is not None
+        ),
+        out_shape=jax.ShapeDtypeStruct(codes.shape, jnp.float32),
+        grid_spec=pltpu.PrefetchScalarGridSpec(
+            num_scalar_prefetch=2,
+            grid=(2, tiles),
+            in_specs=in_specs,
+            out_specs=pl.BlockSpec((1, width, width), tile_of),
+            scratch_shapes=[pltpu.VMEM((id_rows, width), jnp.float32)],
+        ),
+        input_output_aliases=aliases,
+        compiler_params=pltpu.CompilerParams(vmem_limit_bytes=40 * 2**20),
+        cost_estimate=pl.CostEstimate(
+            flops=4 * B * B * width, bytes_accessed=5 * 2 * B * width * 4, transcendentals=0
+        ),
+        name="fold",
+    )(*operands)
+
+
+def shards(grad, owner, codes, scale_ids, scale_table):
+    width = grad.shape[1]
+    slot_count = grad.shape[0] // B
+    group_size = B // width
+    tensor_pos = lax.axis_index("tensor")
+    fsdp_pos = lax.axis_index("fsdp")
+    member = fsdp_pos % group_size
+    column = fsdp_pos // group_size
+    pieces = grad.reshape(slot_count, B, width)
+
+    by_home = owner.reshape(-1, 2, slot_count)
+    home = jnp.arange(2, dtype=jnp.int32)[None, :, None]
+    leaves = (by_home // slot_count != home).astype(jnp.int32)
+    order = jnp.argsort(leaves, axis=2, stable=True).astype(jnp.int32)
+    leaving = jnp.sum(leaves, axis=2)[:, 0]
+    most_leaving = jnp.max(leaving)
+    my_order = order[column, tensor_pos]
+    staying = slot_count - leaving[column]
+    source = jnp.where(jnp.arange(slot_count) < staying, tensor_pos, 1 - tensor_pos)
+    my_slots = by_home[column, source, order[column, source, jnp.arange(slot_count)]] % slot_count
+
+    def cross(value):
+        return partner_2(value, "tensor", 0)
+
+    def taken(step):
+        return lax.dynamic_index_in_dim(pieces, my_order[step], 0, keepdims=False)
+
+    first = lax.cond(most_leaving == slot_count, cross, lambda value: value, taken(0))
+    blocks = [jnp.where(staying > 0, taken(0), first)]
+    received = None
+    for step in range(1, slot_count):
+        sent = taken(step)
+        if received is not None:
+            sent, received = lax.optimization_barrier((sent, received))
+        received = cross(sent)
+        blocks.append(jnp.where(step < staying, sent, received))
+    results = []
+    for step, own in enumerate(blocks):
+        if step >= 2:
+            own, results[step - 2] = lax.optimization_barrier((own, results[step - 2]))
+        across = partner_2(own, "fsdp", 1)
+        beside = partner_2(own, "fsdp", 0)
+        diagonal = partner_2(across, "fsdp", 0)
+        place = jnp.stack([my_slots[step], member]).astype(jnp.int32)
+        filled = results[step - 1] if step > 0 else None
+        results.append(
+            fold(place, scale_table, [own, beside, across, diagonal], codes, scale_ids, filled)
+        )
+    return results[-1]
+
+
 def solution(mesh):
     in_specs = (P("tensor", "fsdp"), P(), P(None, "tensor", "fsdp"), P(None, "tensor", "fsdp"), P())
     out_specs = P(None, "tensor", "fsdp")
-    return jax.shard_map(shards, mesh=mesh, in_specs=in_specs, out_specs=out_specs, check_vma=False)
+
+    def update(grad, owner, codes, scale_ids, scale_table):
+        width = grad.shape[1] // mesh.shape["fsdp"]
+        fits = mesh.shape["tensor"] == 2 and width * 4 == B
+        body = shards if fits else general_shards
+        return jax.shard_map(
+            body, mesh=mesh, in_specs=in_specs, out_specs=out_specs, check_vma=False
+        )(grad, owner, codes, scale_ids, scale_table)
+
+    return update

time: 751 us -> 262 us (0.35)
  waiting for transfers between devices: 373 us -> 152 us
  blocking collectives: 189 us -> 0 us
  other arithmetic: 109 us -> 12.9 us
  matrix products: 67.4 us -> 0 us
  Pallas kernels: 0 us -> 61.1 us
  starting transfers between devices: 1.54 us -> 12.3 us
  between operations: 0.03 us -> 10.5 us
    ppermute x2 -> x15, waiting for transfers between devices: 373 us -> 152 us  [partner_2(): return lax.ppermute(value, axis, pairs)]
    all_to_all x1 -> x0, blocking collectives: 189 us -> none  [shards(): lax.all_to_all(outgoing, 'tensor', split_axis=0, concat_axis=0, tiled=True)]
    dot_general x3 -> x0, matrix products: 67.4 us -> none  [the longest x1 27.5 us: left_part(): jnp.einsum('sbj,scj->sbc', slab_piece, own_rows, preferred_element_type=j...]
    pallas_call x0 -> x4, Pallas kernels: none -> 61.1 us  [fold(): pl.pallas_call(functools.partial(fold_kernel, scale_table.shape[0], group...]
    select_n x2 -> x5, other arithmetic: 55 us -> 7.07 us  [the longest x3 5.51 us: shards(): blocks.append(jnp.where(step < staying, sent, received))]
    add x1 -> x0, other arithmetic: 33.7 us -> none  [shards(): return 0.9 * previous + 0.1 * stacked]
    reduce_sum x2 -> x1, other arithmetic: 20.5 us -> 0.03 us  [shards(): leaving = jnp.sum(leaves, axis=2)[:, 0]]
    ppermute x2 -> x15, starting transfers between devices: 1.54 us -> 12.3 us  [partner_2(): return lax.ppermute(value, axis, pairs)]
  transfers between devices with their start and end apart: 2 -> 15, of which waited for: 2 -> 7; matrix products, arithmetic and copies ran while one was open for 0% -> 6% of each run, Pallas kernels for 0% -> 18%
where the time goes in v1:
time: 262 us; the launch traced here: 260 us
  waiting for transfers between devices  152 us (58%)
  Pallas kernels  61.1 us (23%)
  other arithmetic  12.9 us (5%)
  starting transfers between devices  12.3 us (5%)
  local copies, waits for them, and re-layouts  11.1 us (4%)
  between operations  10.5 us (4%)
    ppermute x15, waiting for transfers between devices, partner_2(): return lax.ppermute(value, axis, pairs)  152 us
    pallas_call x4, Pallas kernels, fold(): pl.pallas_call(functools.partial(fold_kernel, scale_table.shape[0], group...  61.1 us
    ppermute x15, starting transfers between devices, partner_2(): return lax.ppermute(value, axis, pairs)  12.3 us
    squeeze x1, local copies, waits for them, and re-layouts, taken(): return lax.dynamic_index_in_dim(pieces, my_order[step], 0, keepdims=False)  6.32 us
    select_n x3, other arithmetic, shards(): blocks.append(jnp.where(step < staying, sent, received))  5.51 us
  transfers between devices with their start and end apart: 15, of which 7 were waited for; matrix products, arithmetic and copies ran while one was open for 6% of the time, Pallas kernels for 18%

profile of v1, /device:TPU:0, one launch (start us, length us, event | category | flops | bytes accessed | tf_op | source)
XLA Modules:
  0.0 260.1 jit_solution(4180929862705089321)
XLA Ops:
  0.0 0.8 reshape.50
  0.9 1.3 sort.17
  10.3 6.3 %dynamic-slice_bitcast_fusion = (bf16[2048,512]{1,0:T(8,128)(2,1)S(1)}, bf16[2048,512]{1,0:T(8,128)(2,1)}, bf16[2048,512]{1,0:T(8,128)(2,1)}, bf16[2048,512]{1,0:T(8,128)(2,1)}) fusion(bf16[4,2048,512]{2,1,0:T(8,128)(2,1)} %bitcast.23, s32[]{:T(128)S(6)} %select_n.121, s32[]{:T(128)S(6)} %select_n.116, s32[]{:T(128)S(6)} %select_n.115, s32[]{:T(128)S(6)} %select_n.114), kind=kLoop, calls=%fused_computation.2 | loop fusion | bytes 16777232 | tf_op jit(solution)/shard_map/jit(dynamic_index_in_dim)/squeeze | solution.py:196
  16.6 3.0 %collective-permute-start.1 = (bf16[2048,512]{1,0:T(8,128)(2,1)}, bf16[2048,512]{1,0:T(8,128)(2,1)}, u32[]{:S(2)}, u32[]{:S(2)}) collective-permute-start(bf16[2048,512]{1,0:T(8,128)(2,1)} %get-tuple-element.25), channel_id=1, source_target_pairs={{0,1},{1,0},{2,3},{3,2},{4,5},{5,4},{6,7},{7,6},{8,9},{9,8},{10,11... | collective-permute-start | bytes 6291464 | tf_op jit(solution)/shard_map/ppermute | solution.py:16
  19.6 0.7 slice_reduce_fusion
  22.0 1.4 conditional.1
  22.1 1.4 copy.28
  23.4 1.6 broadcast_select_fusion.1.refs_0_
  25.0 1.5 collective-permute-start.8
  26.5 39.0 %collective-permute-done.1 = bf16[2048,512]{1,0:T(8,128)(2,1)} collective-permute-done((bf16[2048,512]{1,0:T(8,128)(2,1)}, bf16[2048,512]{1,0:T(8,128)(2,1)}, u32[]{:S(2)}, u32[]{:S(2)}) %collective-permute-start.1) | collective-permute-done | bytes 2097184 | tf_op jit(solution)/shard_map/ppermute | solution.py:16
  65.5 1.7 collective-permute-start.2
  67.8 1.8 broadcast_select_fusion.2.refs_0_
  69.6 1.6 collective-permute-start.5
  71.2 2.4 collective-permute-done.8.refs_2_
  75.3 0.7 gather_fusion
  76.0 36.7 %collective-permute-done.2 = bf16[2048,512]{1,0:T(8,128)(2,1)} collective-permute-done((bf16[2048,512]{1,0:T(8,128)(2,1)}, bf16[2048,512]{1,0:T(8,128)(2,1)}, u32[]{:S(2)}, u32[]{:S(2)}) %collective-permute-start.2) | collective-permute-done | bytes 2097184 | tf_op jit(solution)/shard_map/ppermute | solution.py:16
  112.6 1.4 collective-permute-start.3
  114.1 0.6 gather_fusion.1
  115.3 0.7 pad_add_fusion.2.place
  116.1 1.3 collective-permute-done.5.refs_2_
  118.0 1.9 broadcast_select_fusion.refs_0_
  119.9 17.0 %fold.4.refs_6_ = f32[2,8192,512]{2,1,0:T(8,128)} custom-call(s32[2]{0:T(128)S(1)} %pad_add_fusion.2.place, f32[16]{0:T(128)S(1)} %copy-done.1, bf16[2048,512]{1,0:T(8,128)(2,1)} %broadcast_select_fusion.1.refs_0_, bf16[2048,512]{1,0:T(8,128)(2,1)} %collective-permute-done.7.refs_1_, bf16[2048,512]{1,0:T(8,128)(2,1)} %collective-permute-done.8.refs_2_, ...), custom_call_target="tpu_custom_call" | custom-call | flops 8589934592 | bytes 41943040 | tf_op jit(solution)/shard_map/fold/pallas_call | solution.py:150
  136.9 1.5 collective-permute-start.14
  138.4 20.5 %collective-permute-done.3 = bf16[2048,512]{1,0:T(8,128)(2,1)} collective-permute-done((bf16[2048,512]{1,0:T(8,128)(2,1)}, bf16[2048,512]{1,0:T(8,128)(2,1)}, u32[]{:S(2)}, u32[]{:S(2)}) %collective-permute-start.3) | collective-permute-done | bytes 2097184 | tf_op jit(solution)/shard_map/ppermute | solution.py:16
  158.8 1.8 broadcast_select_fusion.3.refs_0_
  160.7 15.1 %fold.5.refs_6_ = f32[2,8192,512]{2,1,0:T(8,128)} custom-call(s32[2]{0:T(128)S(1)} %pad_add_fusion.1.place, f32[16]{0:T(128)S(1)} %copy-done.1, bf16[2048,512]{1,0:T(8,128)(2,1)S(1)} %broadcast_select_fusion.2.refs_0_, bf16[2048,512]{1,0:T(8,128)(2,1)S(1)} %collective-permute-done.4.refs_1_, ...), custom_call_target="tpu_custom_call", output_to_operand_aliasing={{}: (8, {})} | custom-call | flops 8589934592 | bytes 41943040 | tf_op jit(solution)/shard_map/fold/pallas_call | solution.py:150
  175.8 1.1 collective-permute-start.11
  176.9 8.4 %collective-permute-done.14.refs_2_ = bf16[2048,512]{1,0:T(8,128)(2,1)S(1)} collective-permute-done((bf16[2048,512]{1,0:T(8,128)(2,1)S(1)}, bf16[2048,512]{1,0:T(8,128)(2,1)S(1)}, u32[]{:S(2)}, u32[]{:S(2)}) %collective-permute-start.14) | collective-permute-done | bytes 2097184 | tf_op jit(solution)/shard_map/ppermute | solution.py:16
  185.8 44.0 %collective-permute-done.11.refs_2_ = bf16[2048,512]{1,0:T(8,128)(2,1)S(1)} collective-permute-done((bf16[2048,512]{1,0:T(8,128)(2,1)S(1)}, bf16[2048,512]{1,0:T(8,128)(2,1)S(1)}, u32[]{:S(2)}, u32[]{:S(2)}) %collective-permute-start.11) | collective-permute-done | bytes 2097184 | tf_op jit(solution)/shard_map/ppermute | solution.py:16
  229.9 1.3 pad_add_fusion
  231.2 14.6 %fold.6.refs_6_ = f32[2,8192,512]{2,1,0:T(8,128)} custom-call(s32[2]{0:T(128)S(1)} %get-tuple-element.39.place, f32[16]{0:T(128)S(1)} %copy-done.1, bf16[2048,512]{1,0:T(8,128)(2,1)S(1)} %broadcast_select_fusion.refs_0_, bf16[2048,512]{1,0:T(8,128)(2,1)S(1)} %collective-permute-done.13.refs_1_, ...), custom_call_target="tpu_custom_call", output_to_operand_aliasing={{}: (8, {})} | custom-call | flops 8589934592 | bytes 41943040 | tf_op jit(solution)/shard_map/fold/pallas_call | solution.py:150
  245.8 14.4 %fold.7 = f32[2,8192,512]{2,1,0:T(8,128)} custom-call(s32[2]{0:T(128)S(1)} %get-tuple-element.38.place, f32[16]{0:T(128)S(1)} %copy-done.1, bf16[2048,512]{1,0:T(8,128)(2,1)S(1)} %broadcast_select_fusion.3.refs_0_, bf16[2048,512]{1,0:T(8,128)(2,1)S(1)} %collective-permute-done.10.refs_1_, ...), custom_call_target="tpu_custom_call", output_to_operand_aliasing={{}: (8, {})} | custom-call | flops 8589934592 | bytes 41943040 | tf_op jit(solution)/shard_map/fold/pallas_call | solution.py:150
  (33 shorter events, 3.7 us)
Async XLA Ops:
  16.6 48.9 %collective-permute-start.1 = (bf16[2048,512]{1,0:T(8,128)(2,1)}, bf16[2048,512]{1,0:T(8,128)(2,1)}, u32[]{:S(2)}, u32[]{:S(2)}) collective-permute-start(bf16[2048,512]{1,0:T(8,128)(2,1)} %get-tuple-element.25), channel_id=1, source_target_pairs={{0,1},{1,0},{2,3},{3,2},{4,5},{5,4},{6,7},{7,6},{8,9},{9,8},{10,11... | collective-permute-start | bytes 6291464 | tf_op jit(solution)/shard_map/ppermute | solution.py:16
  25.0 48.6 %collective-permute-start.8 = (bf16[2048,512]{1,0:T(8,128)(2,1)}, bf16[2048,512]{1,0:T(8,128)(2,1)}, u32[]{:S(2)}, u32[]{:S(2)}) collective-permute-start(bf16[2048,512]{1,0:T(8,128)(2,1)} %broadcast_select_fusion.1.refs_0_), channel_id=1, source_target_pairs={{0,4},{2,6},{4,0},{6,2},{8,12},{10,14},{12,8},{14,10},{16,20},{18,... | collective-permute-start | bytes 6291464 | tf_op jit(solution)/shard_map/ppermute | solution.py:16
  65.5 47.1 %collective-permute-start.2 = (bf16[2048,512]{1,0:T(8,128)(2,1)}, bf16[2048,512]{1,0:T(8,128)(2,1)}, u32[]{:S(2)}, u32[]{:S(2)}) collective-permute-start(bf16[2048,512]{1,0:T(8,128)(2,1)} %get-tuple-element.16), channel_id=1, source_target_pairs={{0,1},{1,0},{2,3},{3,2},{4,5},{5,4},{6,7},{7,6},{8,9},{9,8},{10,11... | collective-permute-start | bytes 6291464 | tf_op jit(solution)/shard_map/ppermute | solution.py:16
  69.6 47.7 %collective-permute-start.5 = (bf16[2048,512]{1,0:T(8,128)(2,1)S(1)}, bf16[2048,512]{1,0:T(8,128)(2,1)}, u32[]{:S(2)}, u32[]{:S(2)}) collective-permute-start(bf16[2048,512]{1,0:T(8,128)(2,1)S(1)} %broadcast_select_fusion.2.refs_0_), channel_id=1, source_target_pairs={{0,4},{2,6},{4,0},{6,2},{8,12},{10,14},{12,8},{14,10},{16,20},{18,... | collective-permute-start | bytes 6291464 | tf_op jit(solution)/shard_map/ppermute | solution.py:16
  71.2 48.7 %collective-permute-start.7 = (bf16[2048,512]{1,0:T(8,128)(2,1)}, bf16[2048,512]{1,0:T(8,128)(2,1)}, u32[]{:S(2)}, u32[]{:S(2)}) collective-permute-start(bf16[2048,512]{1,0:T(8,128)(2,1)} %broadcast_select_fusion.1.refs_0_), channel_id=1, source_target_pairs={{0,2},{2,0},{4,6},{6,4},{8,10},{10,8},{12,14},{14,12},{16,18},{18,... | collective-permute-start | bytes 6291464 | tf_op jit(solution)/shard_map/ppermute | solution.py:16
  73.6 46.2 %collective-permute-start.9 = (bf16[2048,512]{1,0:T(8,128)(2,1)}, bf16[2048,512]{1,0:T(8,128)(2,1)}, u32[]{:S(2)}, u32[]{:S(2)}) collective-permute-start(bf16[2048,512]{1,0:T(8,128)(2,1)} %collective-permute-done.8.refs_2_), channel_id=1, source_target_pairs={{0,2},{2,0},{4,6},{6,4},{8,10},{10,8},{12,14},{14,12},{16,18},{18,... | collective-permute-start | bytes 6291464 | tf_op jit(solution)/shard_map/ppermute | solution.py:16
  112.6 46.2 %collective-permute-start.3 = (bf16[2048,512]{1,0:T(8,128)(2,1)}, bf16[2048,512]{1,0:T(8,128)(2,1)}, u32[]{:S(2)}, u32[]{:S(2)}) collective-permute-start(bf16[2048,512]{1,0:T(8,128)(2,1)} %get-tuple-element.17), channel_id=1, source_target_pairs={{0,1},{1,0},{2,3},{3,2},{4,5},{5,4},{6,7},{7,6},{8,9},{9,8},{10,11... | collective-permute-start | bytes 6291464 | tf_op jit(solution)/shard_map/ppermute | solution.py:16
  116.0 44.6 %collective-permute-start.4 = (bf16[2048,512]{1,0:T(8,128)(2,1)S(1)}, bf16[2048,512]{1,0:T(8,128)(2,1)S(1)}, u32[]{:S(2)}, u32[]{:S(2)}) collective-permute-start(bf16[2048,512]{1,0:T(8,128)(2,1)S(1)} %broadcast_select_fusion.2.refs_0_), channel_id=1, source_target_pairs={{0,2},{2,0},{4,6},{6,4},{8,10},{10,8},{12,14},{14,12},{16,18},{18,... | collective-permute-start | bytes 6291464 | tf_op jit(solution)/shard_map/ppermute | solution.py:16
  117.3 43.4 %collective-permute-start.6 = (bf16[2048,512]{1,0:T(8,128)(2,1)}, bf16[2048,512]{1,0:T(8,128)(2,1)S(1)}, u32[]{:S(2)}, u32[]{:S(2)}) collective-permute-start(bf16[2048,512]{1,0:T(8,128)(2,1)} %collective-permute-done.5.refs_2_), channel_id=1, source_target_pairs={{0,2},{2,0},{4,6},{6,4},{8,10},{10,8},{12,14},{14,12},{16,18},{18,... | collective-permute-start | bytes 6291464 | tf_op jit(solution)/shard_map/ppermute | solution.py:16
  118.0 1.9 copy-start
  118.0 1.9 copy-start.1
  119.8 39.0 %copy-start.2 = (bf16[2048,512]{1,0:T(8,128)(2,1)S(1)}, bf16[2048,512]{1,0:T(8,128)(2,1)}, u32[]{:S(2)}) copy-start(bf16[2048,512]{1,0:T(8,128)(2,1)} %get-tuple-element.17) | copy-start | bytes 6291460
  136.9 48.4 %collective-permute-start.14 = (bf16[2048,512]{1,0:T(8,128)(2,1)S(1)}, bf16[2048,512]{1,0:T(8,128)(2,1)S(1)}, u32[]{:S(2)}, u32[]{:S(2)}) collective-permute-start(bf16[2048,512]{1,0:T(8,128)(2,1)S(1)} %broadcast_select_fusion.refs_0_), channel_id=1, source_target_pairs={{0,4},{2,6},{4,0},{6,2},{8,12},{10,14},{12,8},{14,10},{16,20},{18,... | collective-permute-start | bytes 6291464 | tf_op jit(solution)/shard_map/ppermute | solution.py:16
  175.8 54.0 %collective-permute-start.11 = (bf16[2048,512]{1,0:T(8,128)(2,1)S(1)}, bf16[2048,512]{1,0:T(8,128)(2,1)S(1)}, u32[]{:S(2)}, u32[]{:S(2)}) collective-permute-start(bf16[2048,512]{1,0:T(8,128)(2,1)S(1)} %broadcast_select_fusion.3.refs_0_), channel_id=1, source_target_pairs={{0,4},{2,6},{4,0},{6,2},{8,12},{10,14},{12,8},{14,10},{16,20},{18,... | collective-permute-start | bytes 6291464 | tf_op jit(solution)/shard_map/ppermute | solution.py:16
  176.9 54.3 %collective-permute-start.13 = (bf16[2048,512]{1,0:T(8,128)(2,1)S(1)}, bf16[2048,512]{1,0:T(8,128)(2,1)S(1)}, u32[]{:S(2)}, u32[]{:S(2)}) collective-permute-start(bf16[2048,512]{1,0:T(8,128)(2,1)S(1)} %broadcast_select_fusion.refs_0_), channel_id=1, source_target_pairs={{0,2},{2,0},{4,6},{6,4},{8,10},{10,8},{12,14},{14,12},{16,18},{18,... | collective-permute-start | bytes 6291464 | tf_op jit(solution)/shard_map/ppermute | solution.py:16
  185.3 45.9 %collective-permute-start.15 = (bf16[2048,512]{1,0:T(8,128)(2,1)S(1)}, bf16[2048,512]{1,0:T(8,128)(2,1)S(1)}, u32[]{:S(2)}, u32[]{:S(2)}) collective-permute-start(bf16[2048,512]{1,0:T(8,128)(2,1)S(1)} %collective-permute-done.14.refs_2_), channel_id=1, source_target_pairs={{0,2},{2,0},{4,6},{6,4},{8,10},{10,8},{12,14},{14,12},{16,18},{18,... | collective-permute-start | bytes 6291464 | tf_op jit(solution)/shard_map/ppermute | solution.py:16
  185.3 60.4 %collective-permute-start.10 = (bf16[2048,512]{1,0:T(8,128)(2,1)S(1)}, bf16[2048,512]{1,0:T(8,128)(2,1)S(1)}, u32[]{:S(2)}, u32[]{:S(2)}) collective-permute-start(bf16[2048,512]{1,0:T(8,128)(2,1)S(1)} %broadcast_select_fusion.3.refs_0_), channel_id=1, source_target_pairs={{0,2},{2,0},{4,6},{6,4},{8,10},{10,8},{12,14},{14,12},{16,18},{18,... | collective-permute-start | bytes 6291464 | tf_op jit(solution)/shard_map/ppermute | solution.py:16
  229.9 15.9 %collective-permute-start.12 = (bf16[2048,512]{1,0:T(8,128)(2,1)S(1)}, bf16[2048,512]{1,0:T(8,128)(2,1)S(1)}, u32[]{:S(2)}, u32[]{:S(2)}) collective-permute-start(bf16[2048,512]{1,0:T(8,128)(2,1)S(1)} %collective-permute-done.11.refs_2_), channel_id=1, source_target_pairs={{0,2},{2,0},{4,6},{6,4},{8,10},{10,8},{12,14},{14,12},{16,18},{18,... | collective-permute-start | bytes 6291464 | tf_op jit(solution)/shard_map/ppermute | solution.py:16

commit v2 on v0

--- a/solution.py
+++ b/solution.py
@@ -1,6 +1,10 @@
+import functools
+
 import jax
 import jax.numpy as jnp
 from jax import lax
+from jax.experimental import pallas as pl
+from jax.experimental.pallas import tpu as pltpu
 from jax.sharding import PartitionSpec as P
 
 B = 2048
@@ -21,7 +25,7 @@
     return jnp.einsum("sbj,sbc->sjc", slab_piece, own_piece, preferred_element_type=jnp.float32)
 
 
-def shards(grad, owner, codes, scale_ids, scale_table):
+def general_shards(grad, owner, codes, scale_ids, scale_table):
     rows_here = grad.shape[0]
     width_here = grad.shape[1]
     slot_count = rows_here // B
@@ -68,7 +72,272 @@
     return 0.9 * previous + 0.1 * stacked
 
 
+def plan_kernel(slot_count, group_size, owner, plan):
+    tensor_pos = lax.axis_index("tensor")
+    fsdp_pos = lax.axis_index("fsdp")
+    column = lax.div(fsdp_pos, group_size)
+    columns = owner.shape[0]
+
+    def stays(block_column, block_row, home):
+        slot = owner[block_column, block_row]
+        return ((slot >= slot_count).astype(jnp.int32) == home).astype(jnp.int32)
+
+    all_leave = jnp.int32(0)
+    for block_column in range(columns):
+        kept = sum(stays(block_column, row, 0) for row in range(slot_count))
+        all_leave = jnp.maximum(all_leave, (kept == 0).astype(jnp.int32))
+    first_row = tensor_pos * slot_count
+    staying = sum(stays(column, first_row + row, tensor_pos) for row in range(slot_count))
+    keep_at, leave_at = jnp.int32(0), staying
+    for row in range(slot_count):
+        kept = stays(column, first_row + row, tensor_pos)
+        place = jnp.where(kept == 1, keep_at, leave_at)
+        plan[place] = jnp.int32(row)
+
+        @pl.when(kept == 1)
+        def _():
+            plan[slot_count + place] = owner[column, first_row + row] - first_row
+
+        keep_at, leave_at = keep_at + kept, leave_at + 1 - kept
+    arrive_at = staying
+    other_row = slot_count - first_row
+    for row in range(slot_count):
+        comes = stays(column, other_row + row, tensor_pos)
+
+        @pl.when(comes == 1)
+        def _():
+            plan[slot_count + arrive_at] = owner[column, other_row + row] - first_row
+
+        arrive_at = arrive_at + comes
+    plan[2 * slot_count] = staying
+    plan[2 * slot_count + 1] = all_leave
+    plan[2 * slot_count + 2] = lax.rem(fsdp_pos, group_size)
+    plan[2 * slot_count + 3] = jnp.int32(0)
+
+
+def make_plan(owner, slot_count, group_size):
+    return pl.pallas_call(
+        functools.partial(plan_kernel, slot_count, group_size),
+        out_shape=jax.ShapeDtypeStruct((2 * slot_count + 4,), jnp.int32),
+        in_specs=[pl.BlockSpec(memory_space=pltpu.SMEM)],
+        out_specs=pl.BlockSpec(memory_space=pltpu.SMEM),
+        name="plan",
+    )(owner)
+
+
+def fold_kernel(levels, group_rows, slot_count, positions, cuts, plan, table, *refs):
+    count = len(positions)
+    adds = positions[0] != 0
+    piece_refs = [refs[i * cuts : (i + 1) * cuts] for i in range(count)]
+    own_refs = refs[count * cuts : (count + 1) * cuts] if adds else piece_refs[0]
+    codes, ids = refs[(count + adds) * cuts : (count + adds) * cuts + 2]
+    filled = refs[-3]
+    out, strips = refs[-2:]
+    width = codes.shape[2]
+    tiles = B // width
+    chunk_tiles = tiles // cuts
+    item = pl.program_id(0)
+    member = plan[2 * slot_count + 2]
+    member_chunk = lax.div(member, chunk_tiles)
+    member_rows = pl.ds(pl.multiple_of(lax.rem(member, chunk_tiles) * width, width), width)
+
+    for cut in range(cuts):
+
+        @pl.when((item == 0) & (member_chunk == cut))
+        def _():
+            for place, piece in enumerate(piece_refs):
+                strips[place] = piece[cut][member_rows, :]
+
+    def blend(gram, out_tile):
+        wanted = ids[0, pl.ds(0, ids.shape[1]), :]
+        found = jnp.zeros(wanted.shape, jnp.float32)
+        for level in range(levels):
+            found = jnp.where(wanted == level, table[level], found)
+        found = found * (0.9 / 7.5)
+        groups = width // group_rows
+        for tile in range(tiles):
+
+            @pl.when(out_tile == tile)
+            def _():
+                for group in range(groups):
+                    rows = pl.ds(group * group_rows, group_rows)
+                    line = tile * groups + group
+                    stored = found[line : line + 1] * (codes[0, rows, :].astype(jnp.float32) - 7.5)
+                    out[0, rows, :] = (
+                        stored + 0.1 * gram[group * group_rows : (group + 1) * group_rows]
+                    )
+
+    for cut in range(cuts):
+
+        @pl.when((item >= cut * chunk_tiles) & (item < (cut + 1) * chunk_tiles))
+        def _():
+            first = pl.multiple_of((item - cut * chunk_tiles) * width, width)
+            gram = None
+            for place, piece in enumerate(piece_refs):
+                term = lax.dot_general(
+                    piece[cut][pl.ds(first, width), :],
+                    strips[place],
+                    (((1,), (1,)), ((), ())),
+                    preferred_element_type=jnp.float32,
+                )
+                gram = term if gram is None else gram + term
+            if adds:
+                out[0] = filled[0] + 0.1 * gram
+            else:
+                blend(gram, item)
+
+    for place, piece in enumerate(piece_refs):
+
+        @pl.when(item == tiles + place)
+        def _():
+            gram = None
+            for cut in range(cuts):
+                term = lax.dot_general(
+                    piece[cut][...],
+                    own_refs[cut][...],
+                    (((0,), (0,)), ((), ())),
+                    preferred_element_type=jnp.float32,
+                )
+                gram = term if gram is None else gram + term
+            blend(gram, lax.bitwise_xor(member, positions[place]))
+
+
+def fold(step, plan, scale_table, positions, pieces, codes, scale_ids, filled):
+    width = codes.shape[2]
+    tiles = B // width
+    slot_count = codes.shape[1] // B
+    id_rows = scale_ids.shape[1] // slot_count
+    cuts = len(pieces[0])
+    adds = positions[0] != 0
+
+    def tile_of(item, plan, table):
+        right = item >= tiles
+        placed = jnp.where(right, plan[2 * slot_count + 2] ^ (item - tiles + positions[0]), item)
+        return right.astype(jnp.int32), plan[slot_count + step] * tiles + placed, 0
+
+    def code_of(item, plan, table):
+        return tile_of(jnp.maximum(item, tiles) if adds else item, plan, table)
+
+    def filled_of(item, plan, table):
+        return tile_of(jnp.minimum(item, tiles - 1), plan, table)
+
+    def ids_of(item, plan, table):
+        right = jnp.maximum(item, tiles) >= tiles if adds else item >= tiles
+        return right.astype(jnp.int32), plan[slot_count + step], 0
+
+    operands = [plan, scale_table]
+    in_specs = []
+    for piece in pieces:
+        for chunk in piece:
+            in_specs.append(
+                pl.BlockSpec(chunk.shape, lambda *_: (0, 0), pipeline_mode=pl.Buffered(1))
+            )
+            operands.append(chunk)
+    in_specs.append(pl.BlockSpec((1, width, width), code_of))
+    in_specs.append(pl.BlockSpec((1, id_rows, width), ids_of))
+    operands += [codes, scale_ids]
+    aliases = {}
+    if filled is not None:
+        if adds:
+            in_specs.append(pl.BlockSpec((1, width, width), filled_of))
+        else:
+            in_specs.append(pl.BlockSpec(memory_space=pl.ANY))
+        aliases = {len(operands): 0}
+        operands.append(filled)
+    count = len(positions)
+    return pl.pallas_call(
+        functools.partial(
+            fold_kernel, scale_table.shape[0], B // id_rows, slot_count, positions, cuts
+        ),
+        out_shape=jax.ShapeDtypeStruct(codes.shape, jnp.float32),
+        grid_spec=pltpu.PrefetchScalarGridSpec(
+            num_scalar_prefetch=2,
+            grid=(tiles + count,),
+            in_specs=in_specs,
+            out_specs=pl.BlockSpec((1, width, width), tile_of),
+            scratch_shapes=[pltpu.VMEM((count, width, width), jnp.bfloat16)],
+        ),
+        input_output_aliases=aliases,
+        compiler_params=pltpu.CompilerParams(vmem_limit_bytes=40 * 2**20),
+        cost_estimate=pl.CostEstimate(
+            flops=B * B * width * count,
+            bytes_accessed=(tiles + count) * width * width * 8,
+            transcendentals=0,
+        ),
+        name="fold",
+    )(*operands)
+
+
+CUTS = 2
+
+
+def shards(grad, owner, codes, scale_ids, scale_table):
+    width = grad.shape[1]
+    slot_count = grad.shape[0] // B
+    chunk_rows = B // CUTS
+    plan = make_plan(owner, slot_count, B // width)
+    staying = plan[2 * slot_count]
+
+    def cross(value):
+        return partner_2(value, "tensor", 0)
+
+    def taken(index, cut):
+        return lax.dynamic_slice_in_dim(grad, index * B + cut * chunk_rows, chunk_rows, 0)
+
+    def exchanged(index):
+        chunks = [taken(index, cut) for cut in range(CUTS)]
+        return [jnp.where(staying > 0, chunk, cross(chunk)) for chunk in chunks]
+
+    def kept(index):
+        return [taken(index, cut) for cut in range(CUTS)]
+
+    blocks = [lax.cond(plan[2 * slot_count + 1] == 1, exchanged, kept, plan[0])]
+    arrived = []
+    for step in range(1, slot_count):
+        block = []
+        for cut in range(CUTS):
+            index = plan[step]
+            if len(arrived) >= 2:
+                index, arrived[-2] = lax.optimization_barrier((index, arrived[-2]))
+            sent = taken(index, cut)
+            arrived.append(cross(sent))
+            block.append((sent, len(arrived) - 1))
+        blocks.append(block)
+    result = None
+    for step, block in enumerate(blocks):
+        if step == 0:
+            own = list(block)
+        else:
+            own = [jnp.where(step < staying, sent, arrived[place]) for sent, place in block]
+        last = step == slot_count - 1
+        across = [partner_2(chunk, "fsdp", 1) for chunk in own]
+        beside = [partner_2(chunk, "fsdp", 0) for chunk in own]
+        if result is not None:
+            across[0], result = lax.optimization_barrier((across[0], result))
+        if last:
+            result = fold(
+                step, plan, scale_table, (0, 1), [own, beside], codes, scale_ids, result
+            )
+            across[-1], result = lax.optimization_barrier((across[-1], result))
+        diagonal = [partner_2(chunk, "fsdp", 0) for chunk in across]
+        if last:
+            positions, pieces = (2, 3), [across, diagonal, own]
+        else:
+            positions, pieces = (0, 1, 2, 3), [own, beside, across, diagonal]
+        result = fold(step, plan, scale_table, positions, pieces, codes, scale_ids, result)
+    return result
+
+
 def solution(mesh):
     in_specs = (P("tensor", "fsdp"), P(), P(None, "tensor", "fsdp"), P(None, "tensor", "fsdp"), P())
     out_specs = P(None, "tensor", "fsdp")
-    return jax.shard_map(shards, mesh=mesh, in_specs=in_specs, out_specs=out_specs, check_vma=False)
+
+    def update(grad, owner, codes, scale_ids, scale_table):
+        width = grad.shape[1] // mesh.shape["fsdp"]
+        fits = mesh.shape["tensor"] == 2 and width * 4 == B
+        body = shards if fits else general_shards
+        return jax.shard_map(
+            body, mesh=mesh, in_specs=in_specs, out_specs=out_specs, check_vma=False
+        )(grad, owner, codes, scale_ids, scale_table)
+
+    return update

time: 751 us -> 232 us (0.31)
  waiting for transfers between devices: 373 us -> 100 us
  blocking collectives: 189 us -> 0 us
  other arithmetic: 109 us -> 8.18 us
  Pallas kernels: 0 us -> 75.2 us
  matrix products: 67.4 us -> 0 us
  starting transfers between devices: 1.54 us -> 19.1 us
  local copies, waits for them, and re-layouts: 9.23 us -> 18 us
    ppermute x2 -> x30, waiting for transfers between devices: 373 us -> 100 us  [partner_2(): return lax.ppermute(value, axis, pairs)]
    all_to_all x1 -> x0, blocking collectives: 189 us -> none  [shards(): lax.all_to_all(outgoing, 'tensor', split_axis=0, concat_axis=0, tiled=True)]
    pallas_call x0 -> x6, Pallas kernels: none -> 75.2 us  [the longest x5 73.8 us: fold(): pl.pallas_call(functools.partial(fold_kernel, scale_table.shape[0], B //...]
    dot_general x3 -> x0, matrix products: 67.4 us -> none  [the longest x1 27.5 us: left_part(): jnp.einsum('sbj,scj->sbc', slab_piece, own_rows, preferred_element_type=j...]
    select_n x2 -> x6, other arithmetic: 55 us -> 8.18 us  [shards(): jnp.where(step < staying, sent, arrived[place])]
    add x1 -> x0, other arithmetic: 33.7 us -> none  [shards(): return 0.9 * previous + 0.1 * stacked]
    reduce_sum x2 -> x0, other arithmetic: 20.5 us -> none  [the longest x1 19.2 us: shards(): jnp.sum(incoming, axis=0, dtype=jnp.float32).astype(jnp.bfloat16)]
    ppermute x2 -> x30, starting transfers between devices: 1.54 us -> 19.1 us  [partner_2(): return lax.ppermute(value, axis, pairs)]
  transfers between devices with their start and end apart: 2 -> 30, of which waited for: 2 -> 13; matrix products, arithmetic and copies ran while one was open for 0% -> 6% of each run, Pallas kernels for 0% -> 28%
where the time goes in v2:
time: 232 us; the launch traced here: 227 us
  waiting for transfers between devices  100 us (43%)
  Pallas kernels  75.2 us (32%)
  starting transfers between devices  19.1 us (8%)
  local copies, waits for them, and re-layouts  18 us (8%)
  other arithmetic  8.18 us (4%)
  between operations  6.06 us (3%)
    ppermute x30, waiting for transfers between devices, partner_2(): return lax.ppermute(value, axis, pairs)  100 us
    pallas_call x5, Pallas kernels, fold(): pl.pallas_call(functools.partial(fold_kernel, scale_table.shape[0], B //...  73.8 us
    ppermute x30, starting transfers between devices, partner_2(): return lax.ppermute(value, axis, pairs)  19.1 us
    dynamic_slice x4, local copies, waits for them, and re-layouts, taken(): lax.dynamic_slice_in_dim(grad, index * B + cut * chunk_rows, chunk_rows, 0)  9.02 us
    select_n x6, other arithmetic, shards(): jnp.where(step < staying, sent, arrived[place])  8.18 us
    unnamed x30, local copies, waits for them, and re-layouts  7.48 us
  transfers between devices with their start and end apart: 30, of which 13 were waited for; matrix products, arithmetic and copies ran while one was open for 6% of the time, Pallas kernels for 28%

profile of v2, /device:TPU:0, one launch (start us, length us, event | category | flops | bytes accessed | tf_op | source)
XLA Modules:
  0.0 227.4 jit_solution(994081805481121796)
XLA Ops:
  1.3 1.5 fusion
  3.4 3.7 %conditional.1 = (bf16[1024,512]{1,0:T(8,128)(2,1)}, bf16[1024,512]{1,0:T(8,128)(2,1)}) conditional(s32[]{:T(128)} %bitcast.4, (s32[]{:T(128)}, bf16[8192,512]{1,0:T(8,128)(2,1)}) %tuple.25, (s32[]{:T(128)}, s32[]{:T(128)}, bf16[8192,512]{1,0:T(8,128)(2,1)}) %tuple.26), branch_computations={%region_0.0_spmd, %region_1.2_spmd} | conditional | flops 1048585 | bytes 18874576 | solution.py:294
  4.1 3.0 %constant_dynamic-slice_fusion = (bf16[1024,512]{1,0:T(8,128)(2,1)}, bf16[1024,512]{1,0:T(8,128)(2,1)}) fusion(bf16[8192,512]{1,0:T(8,128)(2,1)} %get-tuple-element.15, s32[]{:T(128)S(6)} %select_n.51, s32[]{:T(128)S(6)} %select_n.50), kind=kLoop, calls=%fused_computation | loop fusion | bytes 4194312 | tf_op jit(solution)/shard_map/cond/branch_0_fun/dynamic_slice | solution.py:285
  7.1 2.9 %collective-permute-start.16 = (bf16[1024,512]{1,0:T(8,128)(2,1)}, bf16[1024,512]{1,0:T(8,128)(2,1)S(1)}, u32[]{:S(2)}, u32[]{:S(2)}) collective-permute-start(bf16[1024,512]{1,0:T(8,128)(2,1)} %get-tuple-element.45.refs_0_), channel_id=1, source_target_pairs={{0,4},{2,6},{4,0},{6,2},{8,12},{10,14},{12,8},{14,10},{16,20},{18,... | collective-permute-start | bytes 3145736 | tf_op jit(solution)/shard_map/ppermute | solution.py:16
  10.7 1.7 constant_dynamic-slice_fusion.6
  12.4 2.1 collective-permute-start.2
  14.6 19.6 %collective-permute-done.16.refs_4_ = bf16[1024,512]{1,0:T(8,128)(2,1)S(1)} collective-permute-done((bf16[1024,512]{1,0:T(8,128)(2,1)}, bf16[1024,512]{1,0:T(8,128)(2,1)S(1)}, u32[]{:S(2)}, u32[]{:S(2)}) %collective-permute-start.16) | collective-permute-done | bytes 1048608 | tf_op jit(solution)/shard_map/ppermute | solution.py:16
  34.2 21.7 %collective-permute-done.17.refs_5_ = bf16[1024,512]{1,0:T(8,128)(2,1)} collective-permute-done((bf16[1024,512]{1,0:T(8,128)(2,1)}, bf16[1024,512]{1,0:T(8,128)(2,1)}, u32[]{:S(2)}, u32[]{:S(2)}) %collective-permute-start.17) | collective-permute-done | bytes 1048608 | tf_op jit(solution)/shard_map/ppermute | solution.py:16
  60.3 1.3 broadcast_select_fusion.3.refs_0_
  61.6 1.8 collective-permute-start.13
  63.4 1.7 constant_dynamic-slice_fusion.5
  66.1 1.5 collective-permute-start.3
  73.4 17.7 %fold.5.refs_10_ = f32[2,8192,512]{2,1,0:T(8,128)} custom-call(s32[12]{0:T(128)S(1)} %copy-done.4, f32[16]{0:T(128)S(1)} %copy-done.6, bf16[1024,512]{1,0:T(8,128)(2,1)} %get-tuple-element.45.refs_0_, bf16[1024,512]{1,0:T(8,128)(2,1)} %get-tuple-element.46.refs_1_, bf16[1024,512]{1,0:T(8,128)(2,1)S(1)} %copy-done.3, ...), custom_call_target="tpu_custom_call" | custom-call | flops 8589934592 | bytes 16777216 | tf_op jit(solution)/shard_map/fold/pallas_call | solution.py:248
  92.3 16.6 %collective-permute-done.20.refs_5_ = bf16[1024,512]{1,0:T(8,128)(2,1)} collective-permute-done((bf16[1024,512]{1,0:T(8,128)(2,1)S(1)}, bf16[1024,512]{1,0:T(8,128)(2,1)}, u32[]{:S(2)}, u32[]{:S(2)}) %collective-permute-start.20) | collective-permute-done | bytes 1048608 | tf_op jit(solution)/shard_map/ppermute | solution.py:16
  108.9 4.1 %collective-permute-done.7 = bf16[1024,512]{1,0:T(8,128)(2,1)S(1)} collective-permute-done((bf16[1024,512]{1,0:T(8,128)(2,1)S(1)}, bf16[1024,512]{1,0:T(8,128)(2,1)S(1)}, u32[]{:S(2)}, u32[]{:S(2)}) %collective-permute-start.7) | collective-permute-done | bytes 1048608 | tf_op jit(solution)/shard_map/ppermute | solution.py:16
  115.7 2.7 %constant_dynamic-slice_fusion.4 = (bf16[1024,512]{1,0:T(8,128)(2,1)}, bf16[1024,512]{1,0:T(8,128)(2,1)S(1)}) fusion(bf16[8192,512]{1,0:T(8,128)(2,1)} %param.7, s32[]{:T(128)S(6)} %select_n.85, s32[]{:T(128)S(6)} %select_n.75), kind=kLoop, calls=%fused_computation.12 | loop fusion | bytes 4194312 | tf_op jit(solution)/shard_map/dynamic_slice | solution.py:285
  118.3 2.7 %broadcast_select_fusion.4.refs_1_ = bf16[1024,512]{1,0:T(8,128)(2,1)} fusion(bf16[1024,512]{1,0:T(8,128)(2,1)} %copy-done.8, bf16[1024,512]{1,0:T(8,128)(2,1)} %copy-done.12, pred[]{:T(512)S(6)} %gt.17), kind=kLoop, calls=%fused_computation.8 | loop fusion | flops 524288 | bytes 3145729 | tf_op jit(solution)/shard_map/jit(_where)/select_n | solution.py:311
  121.0 1.7 collective-permute-start.23
  122.8 1.5 collective-permute-start.4
  124.8 15.4 %collective-permute-done.10.refs_4_ = bf16[1024,512]{1,0:T(8,128)(2,1)} collective-permute-done((bf16[1024,512]{1,0:T(8,128)(2,1)S(1)}, bf16[1024,512]{1,0:T(8,128)(2,1)}, u32[]{:S(2)}, u32[]{:S(2)}) %collective-permute-start.10) | collective-permute-done | bytes 1048608 | tf_op jit(solution)/shard_map/ppermute | solution.py:16
  140.2 1.5 collective-permute-start.26
  141.7 17.3 %fold.6.refs_10_ = f32[2,8192,512]{2,1,0:T(8,128)} custom-call(s32[12]{0:T(128)S(1)} %copy-done.5, f32[16]{0:T(128)S(1)} %copy-done.7, bf16[1024,512]{1,0:T(8,128)(2,1)S(1)} %broadcast_select_fusion.3.refs_0_, bf16[1024,512]{1,0:T(8,128)(2,1)S(1)} %broadcast_select_fusion.2.refs_1_, ...), custom_call_target="tpu_custom_call", output_to_operand_aliasing={{}: (12, {})} | custom-call | flops 8589934592 | bytes 16777216 | tf_op jit(solution)/shard_map/fold/pallas_call | solution.py:248
  162.1 1.3 broadcast_select_fusion.7.refs_0_.refs_4_
  163.5 4.7 %collective-permute-done.26 = bf16[1024,512]{1,0:T(8,128)(2,1)} collective-permute-done((bf16[1024,512]{1,0:T(8,128)(2,1)}, bf16[1024,512]{1,0:T(8,128)(2,1)}, u32[]{:S(2)}, u32[]{:S(2)}) %collective-permute-start.26) | collective-permute-done | bytes 1048608 | tf_op jit(solution)/shard_map/ppermute | solution.py:16
  170.5 1.7 collective-permute-start.27
  172.2 17.4 %fold.7.refs_6_ = f32[2,8192,512]{2,1,0:T(8,128)} custom-call(s32[12]{0:T(128)S(1)} %copy-done.5, f32[16]{0:T(128)S(1)} %copy-done.7, bf16[1024,512]{1,0:T(8,128)(2,1)S(1)} %broadcast_select_fusion.5.refs_0_, bf16[1024,512]{1,0:T(8,128)(2,1)} %broadcast_select_fusion.4.refs_1_, ...), custom_call_target="tpu_custom_call", output_to_operand_aliasing={{}: (12, {})} | custom-call | flops 8589934592 | bytes 16777216 | tf_op jit(solution)/shard_map/fold/pallas_call | solution.py:248
  189.6 4.8 %collective-permute-done.5.refs_0_ = bf16[1024,512]{1,0:T(8,128)(2,1)S(1)} collective-permute-done((bf16[1024,512]{1,0:T(8,128)(2,1)S(1)}, bf16[1024,512]{1,0:T(8,128)(2,1)S(1)}, u32[]{:S(2)}, u32[]{:S(2)}) %collective-permute-start.5) | collective-permute-done | bytes 1048608 | tf_op jit(solution)/shard_map/ppermute | solution.py:16
  194.3 11.2 %fold.8.refs_8_ = f32[2,8192,512]{2,1,0:T(8,128)} custom-call(s32[12]{0:T(128)S(1)} %copy-done.5, f32[16]{0:T(128)S(1)} %copy-done.7, bf16[1024,512]{1,0:T(8,128)(2,1)S(1)} %broadcast_select_fusion.7.refs_0_.refs_4_, bf16[1024,512]{1,0:T(8,128)(2,1)S(1)} %broadcast_select_fusion.6.refs_1_.refs_5_, ...), custom_call_target="tpu_custom_call", output_to_operand_aliasing={{}: (8, {})} | custom-call | flops 4294967296 | bytes 12582912 | tf_op jit(solution)/shard_map/fold/pallas_call | solution.py:248
  205.6 7.1 %collective-permute-done.27.refs_1_ = bf16[1024,512]{1,0:T(8,128)(2,1)S(1)} collective-permute-done((bf16[1024,512]{1,0:T(8,128)(2,1)S(1)}, bf16[1024,512]{1,0:T(8,128)(2,1)S(1)}, u32[]{:S(2)}, u32[]{:S(2)}) %collective-permute-start.27) | collective-permute-done | bytes 1048608 | tf_op jit(solution)/shard_map/ppermute | solution.py:16
  213.2 2.1 collective-permute-done.31.refs_3_
  215.4 1.5 collective-permute-done.30.refs_2_
  216.9 10.3 %fold.9 = f32[2,8192,512]{2,1,0:T(8,128)} custom-call(s32[12]{0:T(128)S(1)} %copy-done.5, f32[16]{0:T(128)S(1)} %copy-done.7, bf16[1024,512]{1,0:T(8,128)(2,1)S(1)} %collective-permute-done.5.refs_0_, bf16[1024,512]{1,0:T(8,128)(2,1)S(1)} %collective-permute-done.27.refs_1_, ...), custom_call_target="tpu_custom_call", output_to_operand_aliasing={{}: (10, {})} | custom-call | flops 4294967296 | bytes 12582912 | tf_op jit(solution)/shard_map/fold/pallas_call | solution.py:248
  (76 shorter events, 18.5 us)
Async XLA Ops:
  7.1 27.1 %collective-permute-start.16 = (bf16[1024,512]{1,0:T(8,128)(2,1)}, bf16[1024,512]{1,0:T(8,128)(2,1)S(1)}, u32[]{:S(2)}, u32[]{:S(2)}) collective-permute-start(bf16[1024,512]{1,0:T(8,128)(2,1)} %get-tuple-element.45.refs_0_), channel_id=1, source_target_pairs={{0,4},{2,6},{4,0},{6,2},{8,12},{10,14},{12,8},{14,10},{16,20},{18,... | collective-permute-start | bytes 3145736 | tf_op jit(solution)/shard_map/ppermute | solution.py:16
  10.0 45.9 %collective-permute-start.17 = (bf16[1024,512]{1,0:T(8,128)(2,1)}, bf16[1024,512]{1,0:T(8,128)(2,1)}, u32[]{:S(2)}, u32[]{:S(2)}) collective-permute-start(bf16[1024,512]{1,0:T(8,128)(2,1)} %get-tuple-element.46.refs_1_), channel_id=1, source_target_pairs={{0,4},{2,6},{4,0},{6,2},{8,12},{10,14},{12,8},{14,10},{16,20},{18,... | collective-permute-start | bytes 3145736 | tf_op jit(solution)/shard_map/ppermute | solution.py:16
  12.4 43.5 %collective-permute-start.2 = (bf16[1024,512]{1,0:T(8,128)(2,1)S(1)}, bf16[1024,512]{1,0:T(8,128)(2,1)S(1)}, u32[]{:S(2)}, u32[]{:S(2)}) collective-permute-start(bf16[1024,512]{1,0:T(8,128)(2,1)S(1)} %get-tuple-element.65), channel_id=1, source_target_pairs={{0,1},{1,0},{2,3},{3,2},{4,5},{5,4},{6,7},{7,6},{8,9},{9,8},{10,11... | collective-permute-start | bytes 3145736 | tf_op jit(solution)/shard_map/ppermute | solution.py:16
  14.5 45.2 %collective-permute-start.6 = (bf16[1024,512]{1,0:T(8,128)(2,1)S(1)}, bf16[1024,512]{1,0:T(8,128)(2,1)}, u32[]{:S(2)}, u32[]{:S(2)}) collective-permute-start(bf16[1024,512]{1,0:T(8,128)(2,1)S(1)} %get-tuple-element.64), channel_id=1, source_target_pairs={{0,1},{1,0},{2,3},{3,2},{4,5},{5,4},{6,7},{7,6},{8,9},{9,8},{10,11... | collective-permute-start | bytes 3145736 | tf_op jit(solution)/shard_map/ppermute | solution.py:16
  14.6 50.5 %collective-permute-start.14 = (bf16[1024,512]{1,0:T(8,128)(2,1)}, bf16[1024,512]{1,0:T(8,128)(2,1)S(1)}, u32[]{:S(2)}, u32[]{:S(2)}) collective-permute-start(bf16[1024,512]{1,0:T(8,128)(2,1)} %get-tuple-element.45.refs_0_), channel_id=1, source_target_pairs={{0,2},{2,0},{4,6},{6,4},{8,10},{10,8},{12,14},{14,12},{16,18},{18,... | collective-permute-start | bytes 3145736 | tf_op jit(solution)/shard_map/ppermute | solution.py:16
  34.2 34.8 %collective-permute-start.15 = (bf16[1024,512]{1,0:T(8,128)(2,1)}, bf16[1024,512]{1,0:T(8,128)(2,1)}, u32[]{:S(2)}, u32[]{:S(2)}) collective-permute-start(bf16[1024,512]{1,0:T(8,128)(2,1)} %get-tuple-element.46.refs_1_), channel_id=1, source_target_pairs={{0,2},{2,0},{4,6},{6,4},{8,10},{10,8},{12,14},{14,12},{16,18},{18,... | collective-permute-start | bytes 3145736 | tf_op jit(solution)/shard_map/ppermute | solution.py:16
  55.9 13.1 %collective-permute-start.18 = (bf16[1024,512]{1,0:T(8,128)(2,1)S(1)}, bf16[1024,512]{1,0:T(8,128)(2,1)}, u32[]{:S(2)}, u32[]{:S(2)}) collective-permute-start(bf16[1024,512]{1,0:T(8,128)(2,1)S(1)} %collective-permute-done.16.refs_4_), channel_id=1, source_target_pairs={{0,2},{2,0},{4,6},{6,4},{8,10},{10,8},{12,14},{14,12},{16,18},{18,... | collective-permute-start | bytes 3145736 | tf_op jit(solution)/shard_map/ppermute | solution.py:16
  57.0 12.7 %collective-permute-start.19 = (bf16[1024,512]{1,0:T(8,128)(2,1)}, bf16[1024,512]{1,0:T(8,128)(2,1)}, u32[]{:S(2)}, u32[]{:S(2)}) collective-permute-start(bf16[1024,512]{1,0:T(8,128)(2,1)} %collective-permute-done.17.refs_5_), channel_id=1, source_target_pairs={{0,2},{2,0},{4,6},{6,4},{8,10},{10,8},{12,14},{14,12},{16,18},{18,... | collective-permute-start | bytes 3145736 | tf_op jit(solution)/shard_map/ppermute | solution.py:16
  61.6 29.5 %collective-permute-start.13 = (bf16[1024,512]{1,0:T(8,128)(2,1)S(1)}, bf16[1024,512]{1,0:T(8,128)(2,1)}, u32[]{:S(2)}, u32[]{:S(2)}) collective-permute-start(bf16[1024,512]{1,0:T(8,128)(2,1)S(1)} %broadcast_select_fusion.3.refs_0_), channel_id=1, source_target_pairs={{0,4},{2,6},{4,0},{6,2},{8,12},{10,14},{12,8},{14,10},{16,20},{18,... | collective-permute-start | bytes 3145736 | tf_op jit(solution)/shard_map/ppermute | solution.py:16
  66.1 26.1 %collective-permute-start.3 = (bf16[1024,512]{1,0:T(8,128)(2,1)S(1)}, bf16[1024,512]{1,0:T(8,128)(2,1)S(1)}, u32[]{:S(2)}, u32[]{:S(2)}) collective-permute-start(bf16[1024,512]{1,0:T(8,128)(2,1)S(1)} %get-tuple-element.63), channel_id=1, source_target_pairs={{0,1},{1,0},{2,3},{3,2},{4,5},{5,4},{6,7},{7,6},{8,9},{9,8},{10,11... | collective-permute-start | bytes 3145736 | tf_op jit(solution)/shard_map/ppermute | solution.py:16
  69.0 52.1 %collective-permute-start.11 = (bf16[1024,512]{1,0:T(8,128)(2,1)S(1)}, bf16[1024,512]{1,0:T(8,128)(2,1)}, u32[]{:S(2)}, u32[]{:S(2)}) collective-permute-start(bf16[1024,512]{1,0:T(8,128)(2,1)S(1)} %broadcast_select_fusion.3.refs_0_), channel_id=1, source_target_pairs={{0,2},{2,0},{4,6},{6,4},{8,10},{10,8},{12,14},{14,12},{16,18},{18,... | collective-permute-start | bytes 3145736 | tf_op jit(solution)/shard_map/ppermute | solution.py:16
  69.1 39.8 %collective-permute-start.20 = (bf16[1024,512]{1,0:T(8,128)(2,1)S(1)}, bf16[1024,512]{1,0:T(8,128)(2,1)}, u32[]{:S(2)}, u32[]{:S(2)}) collective-permute-start(bf16[1024,512]{1,0:T(8,128)(2,1)S(1)} %broadcast_select_fusion.2.refs_1_), channel_id=1, source_target_pairs={{0,4},{2,6},{4,0},{6,2},{8,12},{10,14},{12,8},{14,10},{16,20},{18,... | collective-permute-start | bytes 3145736 | tf_op jit(solution)/shard_map/ppermute | solution.py:16
  69.7 43.3 %collective-permute-start.7 = (bf16[1024,512]{1,0:T(8,128)(2,1)S(1)}, bf16[1024,512]{1,0:T(8,128)(2,1)S(1)}, u32[]{:S(2)}, u32[]{:S(2)}) collective-permute-start(bf16[1024,512]{1,0:T(8,128)(2,1)S(1)} %get-tuple-element.62), channel_id=1, source_target_pairs={{0,1},{1,0},{2,3},{3,2},{4,5},{5,4},{6,7},{7,6},{8,9},{9,8},{10,11... | collective-permute-start | bytes 3145736 | tf_op jit(solution)/shard_map/ppermute | solution.py:16
  73.4 68.3 %copy-start.5 = (s32[12]{0:T(128)S(1)}, s32[12]{0:T(128)}, u32[]{:S(2)}) copy-start(s32[12]{0:T(128)} %plan.1) | copy-start | bytes 148
  73.4 68.3 %copy-start.7 = (f32[16]{0:T(128)S(1)}, f32[16]{0:T(128)}, u32[]{:S(2)}) copy-start(f32[16]{0:T(128)} %table.9) | copy-start | bytes 196
  91.1 31.7 %collective-permute-start.12 = (bf16[1024,512]{1,0:T(8,128)(2,1)S(1)}, bf16[1024,512]{1,0:T(8,128)(2,1)}, u32[]{:S(2)}, u32[]{:S(2)}) collective-permute-start(bf16[1024,512]{1,0:T(8,128)(2,1)S(1)} %broadcast_select_fusion.2.refs_1_), channel_id=1, source_target_pairs={{0,2},{2,0},{4,6},{6,4},{8,10},{10,8},{12,14},{14,12},{16,18},{18,... | collective-permute-start | bytes 3145736 | tf_op jit(solution)/shard_map/ppermute | solution.py:16
  92.2 32.1 %collective-permute-start.21 = (bf16[1024,512]{1,0:T(8,128)(2,1)}, bf16[1024,512]{1,0:T(8,128)(2,1)}, u32[]{:S(2)}, u32[]{:S(2)}) collective-permute-start(bf16[1024,512]{1,0:T(8,128)(2,1)} %collective-permute-done.13.refs_4_), channel_id=1, source_target_pairs={{0,2},{2,0},{4,6},{6,4},{8,10},{10,8},{12,14},{14,12},{16,18},{18,... | collective-permute-start | bytes 3145736 | tf_op jit(solution)/shard_map/ppermute | solution.py:16
  108.9 15.4 %collective-permute-start.22 = (bf16[1024,512]{1,0:T(8,128)(2,1)}, bf16[1024,512]{1,0:T(8,128)(2,1)}, u32[]{:S(2)}, u32[]{:S(2)}) collective-permute-start(bf16[1024,512]{1,0:T(8,128)(2,1)} %collective-permute-done.20.refs_5_), channel_id=1, source_target_pairs={{0,2},{2,0},{4,6},{6,4},{8,10},{10,8},{12,14},{14,12},{16,18},{18,... | collective-permute-start | bytes 3145736 | tf_op jit(solution)/shard_map/ppermute | solution.py:16
  114.0 26.2 %collective-permute-start.10 = (bf16[1024,512]{1,0:T(8,128)(2,1)S(1)}, bf16[1024,512]{1,0:T(8,128)(2,1)}, u32[]{:S(2)}, u32[]{:S(2)}) collective-permute-start(bf16[1024,512]{1,0:T(8,128)(2,1)S(1)} %broadcast_select_fusion.5.refs_0_), channel_id=1, source_target_pairs={{0,4},{2,6},{4,0},{6,2},{8,12},{10,14},{12,8},{14,10},{16,20},{18,... | collective-permute-start | bytes 3145736 | tf_op jit(solution)/shard_map/ppermute | solution.py:16
  121.0 39.0 %collective-permute-start.23 = (bf16[1024,512]{1,0:T(8,128)(2,1)}, bf16[1024,512]{1,0:T(8,128)(2,1)}, u32[]{:S(2)}, u32[]{:S(2)}) collective-permute-start(bf16[1024,512]{1,0:T(8,128)(2,1)} %broadcast_select_fusion.4.refs_1_), channel_id=1, source_target_pairs={{0,4},{2,6},{4,0},{6,2},{8,12},{10,14},{12,8},{14,10},{16,20},{18,... | collective-permute-start | bytes 3145736 | tf_op jit(solution)/shard_map/ppermute | solution.py:16
  122.8 37.3 %collective-permute-start.4 = (bf16[1024,512]{1,0:T(8,128)(2,1)S(1)}, bf16[1024,512]{1,0:T(8,128)(2,1)S(1)}, u32[]{:S(2)}, u32[]{:S(2)}) collective-permute-start(bf16[1024,512]{1,0:T(8,128)(2,1)S(1)} %get-tuple-element.61), channel_id=1, source_target_pairs={{0,1},{1,0},{2,3},{3,2},{4,5},{5,4},{6,7},{7,6},{8,9},{9,8},{10,11... | collective-permute-start | bytes 3145736 | tf_op jit(solution)/shard_map/ppermute | solution.py:16
  124.3 45.6 %collective-permute-start.9 = (bf16[1024,512]{1,0:T(8,128)(2,1)}, bf16[1024,512]{1,0:T(8,128)(2,1)}, u32[]{:S(2)}, u32[]{:S(2)}) collective-permute-start(bf16[1024,512]{1,0:T(8,128)(2,1)} %broadcast_select_fusion.4.refs_1_), channel_id=1, source_target_pairs={{0,2},{2,0},{4,6},{6,4},{8,10},{10,8},{12,14},{14,12},{16,18},{18,... | collective-permute-start | bytes 3145736 | tf_op jit(solution)/shard_map/ppermute | solution.py:16
  124.3 45.7 %collective-permute-start.8 = (bf16[1024,512]{1,0:T(8,128)(2,1)S(1)}, bf16[1024,512]{1,0:T(8,128)(2,1)}, u32[]{:S(2)}, u32[]{:S(2)}) collective-permute-start(bf16[1024,512]{1,0:T(8,128)(2,1)S(1)} %broadcast_select_fusion.5.refs_0_), channel_id=1, source_target_pairs={{0,2},{2,0},{4,6},{6,4},{8,10},{10,8},{12,14},{14,12},{16,18},{18,... | collective-permute-start | bytes 3145736 | tf_op jit(solution)/shard_map/ppermute | solution.py:16
  140.2 28.1 %collective-permute-start.26 = (bf16[1024,512]{1,0:T(8,128)(2,1)}, bf16[1024,512]{1,0:T(8,128)(2,1)}, u32[]{:S(2)}, u32[]{:S(2)}) collective-permute-start(bf16[1024,512]{1,0:T(8,128)(2,1)} %get-tuple-element.60), channel_id=1, source_target_pairs={{0,1},{1,0},{2,3},{3,2},{4,5},{5,4},{6,7},{7,6},{8,9},{9,8},{10,11... | collective-permute-start | bytes 3145736 | tf_op jit(solution)/shard_map/ppermute | solution.py:16
  160.0 10.5 %collective-permute-start.24 = (bf16[1024,512]{1,0:T(8,128)(2,1)}, bf16[1024,512]{1,0:T(8,128)(2,1)S(1)}, u32[]{:S(2)}, u32[]{:S(2)}) collective-permute-start(bf16[1024,512]{1,0:T(8,128)(2,1)} %collective-permute-done.10.refs_4_), channel_id=1, source_target_pairs={{0,2},{2,0},{4,6},{6,4},{8,10},{10,8},{12,14},{14,12},{16,18},{18,... | collective-permute-start | bytes 3145736 | tf_op jit(solution)/shard_map/ppermute | solution.py:16
  161.0 11.2 %collective-permute-start.25 = (bf16[1024,512]{1,0:T(8,128)(2,1)}, bf16[1024,512]{1,0:T(8,128)(2,1)}, u32[]{:S(2)}, u32[]{:S(2)}) collective-permute-start(bf16[1024,512]{1,0:T(8,128)(2,1)} %collective-permute-done.23.refs_5_), channel_id=1, source_target_pairs={{0,2},{2,0},{4,6},{6,4},{8,10},{10,8},{12,14},{14,12},{16,18},{18,... | collective-permute-start | bytes 3145736 | tf_op jit(solution)/shard_map/ppermute | solution.py:16
  168.2 26.1 %collective-permute-start.5 = (bf16[1024,512]{1,0:T(8,128)(2,1)S(1)}, bf16[1024,512]{1,0:T(8,128)(2,1)S(1)}, u32[]{:S(2)}, u32[]{:S(2)}) collective-permute-start(bf16[1024,512]{1,0:T(8,128)(2,1)S(1)} %broadcast_select_fusion.7.refs_0_.refs_4_), channel_id=1, source_target_pairs={{0,4},{2,6},{4,0},{6,2},{8,12},{10,14},{12,8},{14,10},{16,20},{18,... | collective-permute-start | bytes 3145736 | tf_op jit(solution)/shard_map/ppermute | solution.py:16
  169.9 24.4 %collective-permute-start.29 = (bf16[1024,512]{1,0:T(8,128)(2,1)S(1)}, bf16[1024,512]{1,0:T(8,128)(2,1)S(1)}, u32[]{:S(2)}, u32[]{:S(2)}) collective-permute-start(bf16[1024,512]{1,0:T(8,128)(2,1)S(1)} %broadcast_select_fusion.6.refs_1_.refs_5_), channel_id=1, source_target_pairs={{0,2},{2,0},{4,6},{6,4},{8,10},{10,8},{12,14},{14,12},{16,18},{18,... | collective-permute-start | bytes 3145736 | tf_op jit(solution)/shard_map/ppermute | solution.py:16
  170.0 24.3 %collective-permute-start.28 = (bf16[1024,512]{1,0:T(8,128)(2,1)S(1)}, bf16[1024,512]{1,0:T(8,128)(2,1)S(1)}, u32[]{:S(2)}, u32[]{:S(2)}) collective-permute-start(bf16[1024,512]{1,0:T(8,128)(2,1)S(1)} %broadcast_select_fusion.7.refs_0_.refs_4_), channel_id=1, source_target_pairs={{0,2},{2,0},{4,6},{6,4},{8,10},{10,8},{12,14},{14,12},{16,18},{18,... | collective-permute-start | bytes 3145736 | tf_op jit(solution)/shard_map/ppermute | solution.py:16
  170.5 42.2 %collective-permute-start.27 = (bf16[1024,512]{1,0:T(8,128)(2,1)S(1)}, bf16[1024,512]{1,0:T(8,128)(2,1)S(1)}, u32[]{:S(2)}, u32[]{:S(2)}) collective-permute-start(bf16[1024,512]{1,0:T(8,128)(2,1)S(1)} %broadcast_select_fusion.6.refs_1_.refs_5_), channel_id=1, source_target_pairs={{0,4},{2,6},{4,0},{6,2},{8,12},{10,14},{12,8},{14,10},{16,20},{18,... | collective-permute-start | bytes 3145736 | tf_op jit(solution)/shard_map/ppermute | solution.py:16
  212.7 2.7 %collective-permute-start.31 = (bf16[1024,512]{1,0:T(8,128)(2,1)S(1)}, bf16[1024,512]{1,0:T(8,128)(2,1)S(1)}, u32[]{:S(2)}, u32[]{:S(2)}) collective-permute-start(bf16[1024,512]{1,0:T(8,128)(2,1)S(1)} %collective-permute-done.27.refs_1_), channel_id=1, source_target_pairs={{0,2},{2,0},{4,6},{6,4},{8,10},{10,8},{12,14},{14,12},{16,18},{18,... | collective-permute-start | bytes 3145736 | tf_op jit(solution)/shard_map/ppermute | solution.py:16
  212.7 4.2 %collective-permute-start.30 = (bf16[1024,512]{1,0:T(8,128)(2,1)S(1)}, bf16[1024,512]{1,0:T(8,128)(2,1)S(1)}, u32[]{:S(2)}, u32[]{:S(2)}) collective-permute-start(bf16[1024,512]{1,0:T(8,128)(2,1)S(1)} %collective-permute-done.5.refs_0_), channel_id=1, source_target_pairs={{0,2},{2,0},{4,6},{6,4},{8,10},{10,8},{12,14},{14,12},{16,18},{18,... | collective-permute-start | bytes 3145736 | tf_op jit(solution)/shard_map/ppermute | solution.py:16
  (13 other events, 230.0 us)
